TPU v7x, 32 devices: a whole 2x2x4 slice. The times are simulated.
32 devices in a mesh: grp: 4 (over z), exp: 4 (over y, core), rep: 2 (over x).
Axes of the slice: x: 2, y: 2, z: 4, core: 2. Of those that a mesh axis runs over, the one named last changes fastest.
Arguments:
- tokens: bfloat16 [512, 2048], P(('rep', 'grp', 'exp')), parts along dimension 0, may hold values from -6 to 6
- expert_ids: int32 [512, 8], P(('rep', 'grp', 'exp')), parts along dimension 0, may hold values from 0 to 15, as said below
- gate_weights: bfloat16 [512, 8], P(('rep', 'grp', 'exp')), parts along dimension 0, may hold values from 0.049804688 to 0.3984375
- w_gate: bfloat16 [16, 2048, 768], P(('grp', 'exp')), may hold values from -0.125 to 0.125
- w_up: bfloat16 [16, 2048, 768], P(('grp', 'exp')), may hold values from -0.125 to 0.125
- w_down: bfloat16 [16, 768, 2048], P(('grp', 'exp')), may hold values from -0.21875 to 0.21875
Outputs:
- combined: float32 [512, 2048], P(('rep', 'grp', 'exp')), parts along dimension 0
There are 2 independent parts, one for each index of `rep`. A program takes and returns all parts, laid end to end along the dimension named above; an argument that names none is the same for every part. Nothing has to cross between parts.
Inputs may be any that keep to these rules, and one draw needn't show every extreme that they name: `expert_ids`: expert x belongs to group x // 4. Each row names 8 different experts, 4 of them in each of two different groups. Of the 16 rows of one device (aligned blocks of 16 rows), at most 16 name experts of any one group and at most 16 name any one expert; in every draw one group is named by 16 rows of every device, and each of its experts by 16 rows of every device.
All inputs are finite; a program needn't handle non-finite values.
Results may differ from a plain program's by a relative error of at most 0.0041.
Values may be sent and summed in bfloat16 or wider, within the bound.
No kernel may reach another device: no remote copies, remote signals or barrier semaphores. Data moves between devices by JAX's collectives and lax.ppermute only.
A program may use at most 64 MiB of HBM per device.

v0:
```python
import functools

import jax
import jax.numpy as jnp
from jax import lax
from jax.experimental import pallas as pl
from jax.experimental.pallas import tpu as pltpu
from jax.sharding import PartitionSpec as P

CORES = 2
LANES = 128
WHOLE_ROWS = 512
VMEM = pl.BlockSpec(memory_space=pltpu.VMEM)
SMEM = pl.BlockSpec(memory_space=pltpu.SMEM)
HBM = pl.BlockSpec(memory_space=pltpu.HBM)


def partner(index, step, count):
    return index ^ step if count & (count - 1) == 0 else (index + step) % count


def move(value, axis, pairs, back):
    return lax.ppermute(value, axis, [(d, s) for s, d in pairs] if back else pairs)


def prep_kernel(ids_ref, gates_ref, tokens_ref, out_ref, ids_held, gates_held, sems):
    model_width = tokens_ref.shape[1]
    copies = [
        pltpu.make_async_copy(ids_ref, ids_held, sems.at[0]),
        pltpu.make_async_copy(gates_ref, gates_held, sems.at[1]),
        pltpu.make_async_copy(tokens_ref, out_ref.at[:, :model_width], sems.at[2]),
    ]
    for copy in copies:
        copy.start()
    copies[0].wait()
    copies[1].wait()
    width = out_ref.shape[1] - model_width
    top_count, rows = ids_held.shape
    ids = ids_held[...]
    gates = gates_held[...].astype(jnp.float32)
    expert = lax.broadcasted_iota(jnp.int32, (width, rows), 0)
    turned = jnp.zeros((width, rows), jnp.float32)
    for k in range(top_count):
        turned += jnp.where(ids[k : k + 1, :] == expert, gates[k : k + 1, :], 0.0)
    same = lax.broadcasted_iota(jnp.int32, (rows, rows), 0) == lax.broadcasted_iota(
        jnp.int32, (rows, rows), 1
    )
    table = lax.dot_general(
        same.astype(jnp.bfloat16),
        turned.astype(jnp.bfloat16),
        (((1,), (1,)), ((), ())),
        preferred_element_type=jnp.float32,
    )
    out_ref[:, model_width:] = table.astype(jnp.bfloat16)
    copies[2].wait()


def prepare(tokens, expert_ids, gate_weights, experts):
    rows, model_width = tokens.shape
    top_count = expert_ids.shape[1]
    width = experts + -experts % LANES
    return pl.pallas_call(
        prep_kernel,
        out_shape=jax.ShapeDtypeStruct((rows, model_width + width), jnp.bfloat16),
        in_specs=[HBM] * 3,
        out_specs=VMEM,
        scratch_shapes=[
            pltpu.VMEM((top_count, rows), jnp.int32),
            pltpu.VMEM((top_count, rows), jnp.bfloat16),
            pltpu.SemaphoreType.DMA((3,)),
        ],
        compiler_params=pltpu.CompilerParams(vmem_limit_bytes=8 << 20),
    )(expert_ids.T, gate_weights.T, tokens)


def load_kernel(parts, *refs):
    sems = refs[-1]
    count = (len(refs) - 2) // 2
    done_ref = refs[2 * count]
    copies = []
    for at in range(count):
        source, target = refs[at].at[0], refs[count + at]
        rows = target.shape[0] // parts
        for part in range(parts):
            piece = pl.ds(part * rows, rows)
            copies.append(
                pltpu.make_async_copy(source.at[piece], target.at[piece], sems.at[at * parts + part])
            )
    for copy in copies:
        copy.start()
    done_ref[...] = jnp.zeros_like(done_ref)
    for copy in copies:
        copy.wait()


def load_weights(*weights):
    parts = 4
    out = [jax.ShapeDtypeStruct(w.shape[1:], w.dtype) for w in weights]
    out.append(jax.ShapeDtypeStruct((8, LANES), jnp.float32))
    return pl.pallas_call(
        functools.partial(load_kernel, parts),
        out_shape=out,
        in_specs=[HBM] * len(weights),
        out_specs=[VMEM] * len(out),
        scratch_shapes=[pltpu.SemaphoreType.DMA((parts * len(weights),))],
        compiler_params=pltpu.CompilerParams(vmem_limit_bytes=43 << 20),
        cost_estimate=pl.CostEstimate(
            flops=0, bytes_accessed=sum(w.size for w in weights) * 2, transcendentals=0
        ),
    )(*weights)


def expert_kernel(rows, mine_ref, x_ref, gate_ref, up_ref, down_ref, *refs):
    out_ref = refs[-1]
    model_width = out_ref.shape[1]

    def body(step, carry):
        part = pl.ds(pl.multiple_of(step * rows, rows), rows)
        x = x_ref[part, :model_width]
        table = x_ref[part, model_width:].astype(jnp.float32)
        lane = lax.broadcasted_iota(jnp.int32, table.shape, 1)
        scale = jnp.sum(jnp.where(lane == mine_ref[0], table, 0.0), axis=1, keepdims=True)
        gate_pre = jnp.dot(x, gate_ref[...], preferred_element_type=jnp.float32)
        up_pre = jnp.dot(x, up_ref[...], preferred_element_type=jnp.float32)
        hidden = (gate_pre / (1.0 + jnp.exp(-gate_pre)) * up_pre).astype(jnp.bfloat16)
        result = jnp.dot(hidden, down_ref[...], preferred_element_type=jnp.float32)
        out_ref[part, :] = (result * scale).astype(out_ref.dtype)
        return carry

    lax.fori_loop(0, x_ref.shape[0] // rows, body, 0)


def expert_rows(mine, model_width, weights, x, out_type, *after):
    total = x.shape[0]
    rows = next(r for r in range(min(total, 256), 0, -1) if total % r == 0)
    hidden_width = weights[0].shape[1]
    return pl.pallas_call(
        functools.partial(expert_kernel, rows),
        out_shape=jax.ShapeDtypeStruct((total, model_width), out_type),
        in_specs=[SMEM] + [VMEM] * 4 + [HBM] * len(after),
        out_specs=VMEM,
        compiler_params=pltpu.CompilerParams(vmem_limit_bytes=16 << 20),
        cost_estimate=pl.CostEstimate(
            flops=6 * total * model_width * hidden_width,
            bytes_accessed=0,
            transcendentals=total * hidden_width,
        ),
    )(mine, x, *weights, *after)


def pack_kernel(count, *refs):
    out_ref, at = refs[-1], 0
    for ref in refs[:count]:
        out_ref[at : at + ref.shape[0], :] = ref[...]
        at += ref.shape[0]


def pack(pieces, *after):
    rows = sum(piece.shape[0] for piece in pieces)
    return pl.pallas_call(
        functools.partial(pack_kernel, len(pieces)),
        out_shape=jax.ShapeDtypeStruct((rows, pieces[0].shape[1]), pieces[0].dtype),
        in_specs=[VMEM] * len(pieces) + [HBM] * len(after),
        out_specs=VMEM,
        compiler_params=pltpu.CompilerParams(vmem_limit_bytes=8 << 20),
    )(*pieces, *after)


def add_kernel(first, *refs):
    out_ref = refs[-1]
    rows = out_ref.shape[0]
    total = None
    for ref in refs[:-1]:
        part = ref[...] if ref.shape[0] == rows else ref[first : first + rows, :]
        part = part.astype(jnp.float32)
        total = part if total is None else total + part
    out_ref[...] = total.astype(out_ref.dtype)


def add_rows(first, rows, out_type, *terms):
    return pl.pallas_call(
        functools.partial(add_kernel, first),
        out_shape=jax.ShapeDtypeStruct((rows, terms[0].shape[1]), out_type),
        in_specs=[VMEM] * len(terms),
        out_specs=VMEM,
        compiler_params=pltpu.CompilerParams(vmem_limit_bytes=8 << 20),
    )(*terms)


def shards(tokens, expert_ids, gate_weights, w_gate, w_up, w_down):
    tok_rows, model_width = tokens.shape
    groups = lax.axis_size("grp")
    owners = lax.axis_size("exp")
    experts = groups * owners
    chips = owners // CORES
    mine = lax.axis_index("grp") * owners + lax.axis_index("exp")

    def along_grp(value, step, back=False):
        return move(value, "grp", [(i, partner(i, step, groups)) for i in range(groups)], back)

    def along_chip(value, step, back=False):
        pairs = [
            (i * CORES + c, partner(i, step, chips) * CORES + c)
            for i in range(chips)
            for c in range(CORES)
        ]
        return move(value, "exp", pairs, back)

    def along_core(value):
        return move(value, "exp", [(i, i ^ 1) for i in range(owners)], False)

    own = prepare(tokens, expert_ids, gate_weights, experts)
    *weights, loaded = load_weights(w_gate, w_up, w_down)
    apply = functools.partial(expert_rows, mine[None], model_width, weights)
    width = groups if experts * tok_rows <= WHOLE_ROWS else 1
    total = None
    for first in range(0, groups, width):
        if first:
            own, total = lax.optimization_barrier((own, total))
        steps = range(first, first + width)
        line = [along_grp(own, g) if g else own for g in steps]
        far = [along_chip(piece, s) for piece in line for s in range(1, chips)]
        near = pack(line)
        near_other = along_core(near)
        far = pack(far, loaded)
        far_other = along_core(far)
        near_kept = apply(near, jnp.float32)
        far_back = along_core(apply(far_other, jnp.bfloat16, near_kept))
        near_back = along_core(apply(near_other, jnp.bfloat16))
        far_kept = apply(far, jnp.float32)
        for at, g in reversed(list(enumerate(steps))):
            terms = []
            for s in range(1, chips):
                start = (at * (chips - 1) + s - 1) * tok_rows
                piece = add_rows(start, tok_rows, jnp.bfloat16, far_kept, far_back)
                terms.append(along_chip(piece, s, True))
            begin = at * tok_rows
            if g:
                piece = add_rows(begin, tok_rows, jnp.bfloat16, near_kept, near_back, *terms)
                piece = along_grp(piece, g, True).astype(jnp.float32)
            else:
                piece = near_kept[begin : begin + tok_rows]
                for term in [near_back[begin : begin + tok_rows]] + terms:
                    piece = piece + term.astype(jnp.float32)
            total = piece if total is None else total + piece
    return total


def solution(mesh):
    return jax.shard_map(
        shards,
        mesh=mesh,
        in_specs=(
            P(("rep", "grp", "exp"), None),
            P(("rep", "grp", "exp"), None),
            P(("rep", "grp", "exp"), None),
            P(("grp", "exp"), None, None),
            P(("grp", "exp"), None, None),
            P(("grp", "exp"), None, None),
        ),
        out_specs=P(("rep", "grp", "exp"), None),
        check_vma=False,
    )
```

profile of v0, /device:TPU:0, one launch (start us, length us, event | category | flops | bytes accessed | tf_op | source)
XLA Modules:
  0.0 52.9 jit_solution(12542791384562200733)
XLA Ops:
  0.0 0.8 %copy-done.4 = bf16[16,2048]{1,0:T(8,128)(2,1)S(1)} copy-done((bf16[16,2048]{1,0:T(8,128)(2,1)S(1)}, bf16[16,2048]{1,0:T(8,128)(2,1)}, u32[]{:S(2)}) %copy-start.4) | copy-done | bytes 65560
  2.5 5.1 %collective-permute-start.2 = (bf16[16,2176]{1,0:T(8,128)(2,1)S(1)}, bf16[16,2176]{1,0:T(8,128)(2,1)S(1)}, u32[]{:S(2)}, u32[]{:S(2)}) collective-permute-start(bf16[16,2176]{1,0:T(8,128)(2,1)S(1)} %shard_map.64.refs_0_), channel_id=1, source_target_pairs={{0,24},{8,16},{16,8},{24,0},{1,25},{9,17},{17,9},{25,1},{2,26},{10... | collective-permute-start | bytes 208904 | tf_op jit(solution)/shard_map/ppermute | solution.py:23
  8.2 1.7 %collective-permute-start.5 = (bf16[16,2176]{1,0:T(8,128)(2,1)S(1)}, bf16[16,2176]{1,0:T(8,128)(2,1)S(1)}, u32[]{:S(2)}, u32[]{:S(2)}) collective-permute-start(bf16[16,2176]{1,0:T(8,128)(2,1)S(1)} %shard_map.64.refs_0_), channel_id=1, source_target_pairs={{0,4},{2,6},{4,0},{6,2},{1,5},{3,7},{5,1},{7,3},{8,12},{10,14},{12... | collective-permute-start | bytes 208904 | tf_op jit(solution)/shard_map/ppermute | solution.py:23
  10.2 1.9 %collective-permute-start.8 = (bf16[16,2176]{1,0:T(8,128)(2,1)S(1)}, bf16[16,2176]{1,0:T(8,128)(2,1)S(1)}, u32[]{:S(2)}, u32[]{:S(2)}) collective-permute-start(bf16[16,2176]{1,0:T(8,128)(2,1)S(1)} %collective-permute-done.2.refs_3_), channel_id=1, source_target_pairs={{0,4},{2,6},{4,0},{6,2},{1,5},{3,7},{5,1},{7,3},{8,12},{10,14},{12... | collective-permute-start | bytes 208904 | tf_op jit(solution)/shard_map/ppermute | solution.py:23
  12.1 1.4 %collective-permute-done.1.refs_2_ = bf16[16,2176]{1,0:T(8,128)(2,1)S(1)} collective-permute-done((bf16[16,2176]{1,0:T(8,128)(2,1)S(1)}, bf16[16,2176]{1,0:T(8,128)(2,1)S(1)}, u32[]{:S(2)}, u32[]{:S(2)}) %collective-permute-start.1) | collective-permute-done | bytes 69664 | tf_op jit(solution)/shard_map/ppermute | solution.py:23
  13.5 1.5 %collective-permute-start.7 = (bf16[16,2176]{1,0:T(8,128)(2,1)S(1)}, bf16[16,2176]{1,0:T(8,128)(2,1)S(1)}, u32[]{:S(2)}, u32[]{:S(2)}) collective-permute-start(bf16[16,2176]{1,0:T(8,128)(2,1)S(1)} %collective-permute-done.1.refs_2_), channel_id=1, source_target_pairs={{0,4},{2,6},{4,0},{6,2},{1,5},{3,7},{5,1},{7,3},{8,12},{10,14},{12... | collective-permute-start | bytes 208904 | tf_op jit(solution)/shard_map/ppermute | solution.py:23
  15.5 3.8 %shard_map.66 = (bf16[2048,768]{1,0:T(8,128)(2,1)S(1)}, bf16[2048,768]{1,0:T(8,128)(2,1)S(1)}, bf16[768,2048]{1,0:T(8,128)(2,1)S(1)}, f32[8,128]{1,0:T(8,128)S(1)}) custom-call(bf16[1,2048,768]{2,1,0:T(8,128)(2,1)} %refs_0_.1, bf16[1,2048,768]{2,1,0:T(8,128)(2,1)} %refs_1_.1, bf16[1,768,2048]{2,1,0:T(8,128)(2,1)} %refs_2_.1), custom_call_target="tpu_custom_call" | custom-call | bytes 9437184 | tf_op jit(solution)/shard_map/pallas_call | solution.py:100
  19.3 1.6 %copy-done = bf16[2048,768]{1,0:T(8,128)(2,1)} copy-done((bf16[2048,768]{1,0:T(8,128)(2,1)}, bf16[2048,768]{1,0:T(8,128)(2,1)S(1)}, u32[]{:S(2)}) %copy-start) | copy-done | bytes 3145752
  20.9 1.7 %copy-done.2 = bf16[768,2048]{1,0:T(8,128)(2,1)} copy-done((bf16[768,2048]{1,0:T(8,128)(2,1)}, bf16[768,2048]{1,0:T(8,128)(2,1)S(1)}, u32[]{:S(2)}) %copy-start.2) | copy-done | bytes 3145752
  22.7 0.7 %shard_map.65.x_ref = bf16[64,2176]{1,0:T(8,128)(2,1)} custom-call(bf16[16,2176]{1,0:T(8,128)(2,1)S(1)} %shard_map.64.refs_0_, bf16[16,2176]{1,0:T(8,128)(2,1)S(1)} %collective-permute-done.refs_1_, bf16[16,2176]{1,0:T(8,128)(2,1)S(1)} %collective-permute-done.1.refs_2_, bf16[16,2176]{1,0:T(8,128)(2,1)S(1)} %collective-permute-done.2.refs_3_), custom_call_target="tpu_custom_call" | custom-call | tf_op jit(solution)/shard_map/pallas_call | solution.py:160
  24.0 1.9 %copy-done.1 = bf16[2048,768]{1,0:T(8,128)(2,1)S(1)} copy-done((bf16[2048,768]{1,0:T(8,128)(2,1)S(1)}, bf16[2048,768]{1,0:T(8,128)(2,1)}, u32[]{:S(2)}) %copy-start.1) | copy-done | bytes 3145752
  25.9 1.9 %copy-done.3 = bf16[768,2048]{1,0:T(8,128)(2,1)S(1)} copy-done((bf16[768,2048]{1,0:T(8,128)(2,1)S(1)}, bf16[768,2048]{1,0:T(8,128)(2,1)}, u32[]{:S(2)}) %copy-start.3) | copy-done | bytes 3145752
  27.8 2.7 %shard_map.67.refs_0_ = f32[64,2048]{1,0:T(8,128)S(1)} custom-call(s32[1]{0:T(128)} %bitcast.mine_ref, bf16[64,2176]{1,0:T(8,128)(2,1)} %shard_map.65.x_ref, bf16[2048,768]{1,0:T(8,128)(2,1)S(1)} %get-tuple-element.9.gate_ref, bf16[2048,768]{1,0:T(8,128)(2,1)S(1)} %copy-done.1, bf16[768,2048]{1,0:T(8,128)(2,1)S(1)} %copy-done.3), custom_call_target="tpu_custom_call" | custom-call | flops 603979776 | tf_op jit(solution)/shard_map/pallas_call | solution.py:137
  30.5 2.8 %shard_map.71 = bf16[64,2048]{1,0:T(8,128)(2,1)S(1)} custom-call(s32[1]{0:T(128)} %bitcast.mine_ref, bf16[64,2176]{1,0:T(8,128)(2,1)} %collective-permute-done.9.x_ref, bf16[2048,768]{1,0:T(8,128)(2,1)S(1)} %get-tuple-element.9.gate_ref, bf16[2048,768]{1,0:T(8,128)(2,1)S(1)} %copy-done.1, bf16[768,2048]{1,0:T(8,128)(2,1)S(1)} %copy-done.3, ...), custom_call_target="tpu_custom_call" | custom-call | flops 603979776 | tf_op jit(solution)/shard_map/pallas_call | solution.py:137
  33.4 2.8 %shard_map.68 = bf16[64,2048]{1,0:T(8,128)(2,1)S(1)} custom-call(s32[1]{0:T(128)} %bitcast.mine_ref, bf16[64,2176]{1,0:T(8,128)(2,1)} %collective-permute-done.3.x_ref, bf16[2048,768]{1,0:T(8,128)(2,1)S(1)} %get-tuple-element.9.gate_ref, bf16[2048,768]{1,0:T(8,128)(2,1)S(1)} %copy-done.1, bf16[768,2048]{1,0:T(8,128)(2,1)S(1)} %copy-done.3), custom_call_target="tpu_custom_call" | custom-call | flops 603979776 | tf_op jit(solution)/shard_map/pallas_call | solution.py:137
  36.7 1.8 %shard_map.70.refs_0_ = f32[64,2048]{1,0:T(8,128)S(1)} custom-call(s32[1]{0:T(128)} %bitcast.mine_ref, bf16[64,2176]{1,0:T(8,128)(2,1)S(1)} %shard_map.69.x_ref, bf16[2048,768]{1,0:T(8,128)(2,1)S(1)} %get-tuple-element.9.gate_ref, bf16[2048,768]{1,0:T(8,128)(2,1)S(1)} %copy-done.1, bf16[768,2048]{1,0:T(8,128)(2,1)S(1)} %copy-done.3), custom_call_target="tpu_custom_call" | custom-call | flops 603979776 | tf_op jit(solution)/shard_map/pallas_call | solution.py:137
  38.5 1.6 %collective-permute-start.11 = (bf16[16,2048]{1,0:T(8,128)(2,1)S(1)}, bf16[16,2048]{1,0:T(8,128)(2,1)S(1)}, u32[]{:S(2)}, u32[]{:S(2)}) collective-permute-start(bf16[16,2048]{1,0:T(8,128)(2,1)S(1)} %shard_map.72), channel_id=1, source_target_pairs={{4,0},{6,2},{0,4},{2,6},{5,1},{7,3},{1,5},{3,7},{12,8},{14,10},{8,... | collective-permute-start | bytes 196616 | tf_op jit(solution)/shard_map/ppermute | solution.py:23
  40.7 1.6 %collective-permute-start.15 = (bf16[16,2048]{1,0:T(8,128)(2,1)S(1)}, bf16[16,2048]{1,0:T(8,128)(2,1)S(1)}, u32[]{:S(2)}, u32[]{:S(2)}) collective-permute-start(bf16[16,2048]{1,0:T(8,128)(2,1)S(1)} %shard_map.76), channel_id=1, source_target_pairs={{4,0},{6,2},{0,4},{2,6},{5,1},{7,3},{1,5},{3,7},{12,8},{14,10},{8,... | collective-permute-start | bytes 196616 | tf_op jit(solution)/shard_map/ppermute | solution.py:23
  43.3 2.8 %collective-permute-start.12 = (bf16[16,2048]{1,0:T(8,128)(2,1)S(1)}, bf16[16,2048]{1,0:T(8,128)(2,1)S(1)}, u32[]{:S(2)}, u32[]{:S(2)}) collective-permute-start(bf16[16,2048]{1,0:T(8,128)(2,1)S(1)} %shard_map.73), channel_id=1, source_target_pairs={{24,0},{16,8},{8,16},{0,24},{25,1},{17,9},{9,17},{1,25},{26,2},{18... | collective-permute-start | bytes 196616 | tf_op jit(solution)/shard_map/ppermute | solution.py:23
  46.1 1.0 %collective-permute-start.14 = (bf16[16,2048]{1,0:T(8,128)(2,1)S(1)}, bf16[16,2048]{1,0:T(8,128)(2,1)S(1)}, u32[]{:S(2)}, u32[]{:S(2)}) collective-permute-start(bf16[16,2048]{1,0:T(8,128)(2,1)S(1)} %shard_map.75), channel_id=1, source_target_pairs={{16,0},{24,8},{0,16},{8,24},{17,1},{25,9},{1,17},{9,25},{18,2},{26... | collective-permute-start | bytes 196616 | tf_op jit(solution)/shard_map/ppermute | solution.py:23
  47.1 1.5 %collective-permute-start.16 = (bf16[16,2048]{1,0:T(8,128)(2,1)S(1)}, bf16[16,2048]{1,0:T(8,128)(2,1)S(1)}, u32[]{:S(2)}, u32[]{:S(2)}) collective-permute-start(bf16[16,2048]{1,0:T(8,128)(2,1)S(1)} %shard_map.77), channel_id=1, source_target_pairs={{8,0},{0,8},{24,16},{16,24},{9,1},{1,9},{25,17},{17,25},{10,2},{2,... | collective-permute-start | bytes 196616 | tf_op jit(solution)/shard_map/ppermute | solution.py:23
  48.6 1.1 %collective-permute-done.12 = bf16[16,2048]{1,0:T(8,128)(2,1)S(1)} collective-permute-done((bf16[16,2048]{1,0:T(8,128)(2,1)S(1)}, bf16[16,2048]{1,0:T(8,128)(2,1)S(1)}, u32[]{:S(2)}, u32[]{:S(2)}) %collective-permute-start.12) | collective-permute-done | bytes 65568 | tf_op jit(solution)/shard_map/ppermute | solution.py:23
  49.7 2.1 %collective-permute-done.14 = bf16[16,2048]{1,0:T(8,128)(2,1)S(1)} collective-permute-done((bf16[16,2048]{1,0:T(8,128)(2,1)S(1)}, bf16[16,2048]{1,0:T(8,128)(2,1)S(1)}, u32[]{:S(2)}, u32[]{:S(2)}) %collective-permute-start.14) | collective-permute-done | bytes 65568 | tf_op jit(solution)/shard_map/ppermute | solution.py:23
  52.2 0.7 %fusion.1 = f32[16,2048]{1,0:T(8,128)} fusion(f32[64,2048]{1,0:T(8,128)S(1)} %shard_map.67.refs_0_, bf16[16,2048]{1,0:T(8,128)(2,1)S(1)} %collective-permute-done.17, bf16[16,2048]{1,0:T(8,128)(2,1)S(1)} %collective-permute-done.16, bf16[16,2048]{1,0:T(8,128)(2,1)S(1)} %collective-permute-done.14, bf16[16,2048]{1,0:T(8,128)(2,1)S(1)} %collective-permute-done.12, ...), kind=kLoop, calls=%fused_computation.2 | loop fusion | flops 327680 | bytes 589824 | tf_op jit(solution)/shard_map/add | solution.py:245
  (42 shorter events, 6.4 us)
Async XLA Ops:
  0.0 0.8 %copy-start.4 = (bf16[16,2048]{1,0:T(8,128)(2,1)S(1)}, bf16[16,2048]{1,0:T(8,128)(2,1)}, u32[]{:S(2)}) copy-start(bf16[16,2048]{1,0:T(8,128)(2,1)} %tokens_ref.1) | copy-start | bytes 196612
  0.8 0.7 %copy-start.5 = (s32[16,8]{0,1:T(8,128)S(1)}, s32[16,8]{0,1:T(8,128)}, u32[]{:S(2)}) copy-start(s32[16,8]{0,1:T(8,128)} %param.7) | copy-start | bytes 1540
  2.5 7.8 %collective-permute-start.2 = (bf16[16,2176]{1,0:T(8,128)(2,1)S(1)}, bf16[16,2176]{1,0:T(8,128)(2,1)S(1)}, u32[]{:S(2)}, u32[]{:S(2)}) collective-permute-start(bf16[16,2176]{1,0:T(8,128)(2,1)S(1)} %shard_map.64.refs_0_), channel_id=1, source_target_pairs={{0,24},{8,16},{16,8},{24,0},{1,25},{9,17},{17,9},{25,1},{2,26},{10... | collective-permute-start | bytes 208904 | tf_op jit(solution)/shard_map/ppermute | solution.py:23
  7.6 5.9 %collective-permute-start.1 = (bf16[16,2176]{1,0:T(8,128)(2,1)S(1)}, bf16[16,2176]{1,0:T(8,128)(2,1)S(1)}, u32[]{:S(2)}, u32[]{:S(2)}) collective-permute-start(bf16[16,2176]{1,0:T(8,128)(2,1)S(1)} %shard_map.64.refs_0_), channel_id=1, source_target_pairs={{0,16},{8,24},{16,0},{24,8},{1,17},{9,25},{17,1},{25,9},{2,18},{10... | collective-permute-start | bytes 208904 | tf_op jit(solution)/shard_map/ppermute | solution.py:23
  7.6 7.4 %collective-permute-start = (bf16[16,2176]{1,0:T(8,128)(2,1)S(1)}, bf16[16,2176]{1,0:T(8,128)(2,1)S(1)}, u32[]{:S(2)}, u32[]{:S(2)}) collective-permute-start(bf16[16,2176]{1,0:T(8,128)(2,1)S(1)} %shard_map.64.refs_0_), channel_id=1, source_target_pairs={{0,8},{8,0},{16,24},{24,16},{1,9},{9,1},{17,25},{25,17},{2,10},{10... | collective-permute-start | bytes 208904 | tf_op jit(solution)/shard_map/ppermute | solution.py:23
  8.2 14.4 %collective-permute-start.5 = (bf16[16,2176]{1,0:T(8,128)(2,1)S(1)}, bf16[16,2176]{1,0:T(8,128)(2,1)S(1)}, u32[]{:S(2)}, u32[]{:S(2)}) collective-permute-start(bf16[16,2176]{1,0:T(8,128)(2,1)S(1)} %shard_map.64.refs_0_), channel_id=1, source_target_pairs={{0,4},{2,6},{4,0},{6,2},{1,5},{3,7},{5,1},{7,3},{8,12},{10,14},{12... | collective-permute-start | bytes 208904 | tf_op jit(solution)/shard_map/ppermute | solution.py:23
  10.2 12.4 %collective-permute-start.8 = (bf16[16,2176]{1,0:T(8,128)(2,1)S(1)}, bf16[16,2176]{1,0:T(8,128)(2,1)S(1)}, u32[]{:S(2)}, u32[]{:S(2)}) collective-permute-start(bf16[16,2176]{1,0:T(8,128)(2,1)S(1)} %collective-permute-done.2.refs_3_), channel_id=1, source_target_pairs={{0,4},{2,6},{4,0},{6,2},{1,5},{3,7},{5,1},{7,3},{8,12},{10,14},{12... | collective-permute-start | bytes 208904 | tf_op jit(solution)/shard_map/ppermute | solution.py:23
  13.5 9.1 %collective-permute-start.7 = (bf16[16,2176]{1,0:T(8,128)(2,1)S(1)}, bf16[16,2176]{1,0:T(8,128)(2,1)S(1)}, u32[]{:S(2)}, u32[]{:S(2)}) collective-permute-start(bf16[16,2176]{1,0:T(8,128)(2,1)S(1)} %collective-permute-done.1.refs_2_), channel_id=1, source_target_pairs={{0,4},{2,6},{4,0},{6,2},{1,5},{3,7},{5,1},{7,3},{8,12},{10,14},{12... | collective-permute-start | bytes 208904 | tf_op jit(solution)/shard_map/ppermute | solution.py:23
  15.0 7.6 %collective-permute-start.6 = (bf16[16,2176]{1,0:T(8,128)(2,1)S(1)}, bf16[16,2176]{1,0:T(8,128)(2,1)S(1)}, u32[]{:S(2)}, u32[]{:S(2)}) collective-permute-start(bf16[16,2176]{1,0:T(8,128)(2,1)S(1)} %collective-permute-done.refs_1_), channel_id=1, source_target_pairs={{0,4},{2,6},{4,0},{6,2},{1,5},{3,7},{5,1},{7,3},{8,12},{10,14},{12... | collective-permute-start | bytes 208904 | tf_op jit(solution)/shard_map/ppermute | solution.py:23
  19.3 1.6 %copy-start = (bf16[2048,768]{1,0:T(8,128)(2,1)}, bf16[2048,768]{1,0:T(8,128)(2,1)S(1)}, u32[]{:S(2)}) copy-start(bf16[2048,768]{1,0:T(8,128)(2,1)S(1)} %get-tuple-element.10.up_ref) | copy-start | bytes 9437188
  20.9 1.7 %copy-start.2 = (bf16[768,2048]{1,0:T(8,128)(2,1)}, bf16[768,2048]{1,0:T(8,128)(2,1)S(1)}, u32[]{:S(2)}) copy-start(bf16[768,2048]{1,0:T(8,128)(2,1)S(1)} %get-tuple-element.11.down_ref) | copy-start | bytes 9437188
  22.7 7.8 %collective-permute-start.9 = (bf16[64,2176]{1,0:T(8,128)(2,1)S(1)}, bf16[64,2176]{1,0:T(8,128)(2,1)}, u32[]{:S(2)}, u32[]{:S(2)}) collective-permute-start(bf16[64,2176]{1,0:T(8,128)(2,1)S(1)} %shard_map.69.x_ref), channel_id=1, source_target_pairs={{0,2},{2,0},{4,6},{6,4},{1,3},{3,1},{5,7},{7,5},{8,10},{10,8},{12,... | collective-permute-start | bytes 835592 | tf_op jit(solution)/shard_map/ppermute | solution.py:23
  23.5 9.9 %collective-permute-start.3 = (bf16[64,2176]{1,0:T(8,128)(2,1)}, bf16[64,2176]{1,0:T(8,128)(2,1)}, u32[]{:S(2)}, u32[]{:S(2)}) collective-permute-start(bf16[64,2176]{1,0:T(8,128)(2,1)} %shard_map.65.x_ref), channel_id=1, source_target_pairs={{0,2},{2,0},{4,6},{6,4},{1,3},{3,1},{5,7},{7,5},{8,10},{10,8},{12,... | collective-permute-start | bytes 835592 | tf_op jit(solution)/shard_map/ppermute | solution.py:23
  24.0 1.9 %copy-start.1 = (bf16[2048,768]{1,0:T(8,128)(2,1)S(1)}, bf16[2048,768]{1,0:T(8,128)(2,1)}, u32[]{:S(2)}) copy-start(bf16[2048,768]{1,0:T(8,128)(2,1)} %copy-done) | copy-start | bytes 9437188
  25.9 1.9 %copy-start.3 = (bf16[768,2048]{1,0:T(8,128)(2,1)S(1)}, bf16[768,2048]{1,0:T(8,128)(2,1)}, u32[]{:S(2)}) copy-start(bf16[768,2048]{1,0:T(8,128)(2,1)} %copy-done.2) | copy-start | bytes 9437188
  33.3 5.2 %collective-permute-start.10 = (bf16[64,2048]{1,0:T(8,128)(2,1)S(1)}, bf16[64,2048]{1,0:T(8,128)(2,1)S(1)}, u32[]{:S(2)}, u32[]{:S(2)}) collective-permute-start(bf16[64,2048]{1,0:T(8,128)(2,1)S(1)} %shard_map.71), channel_id=1, source_target_pairs={{0,2},{2,0},{4,6},{6,4},{1,3},{3,1},{5,7},{7,5},{8,10},{10,8},{12,... | collective-permute-start | bytes 786440 | tf_op jit(solution)/shard_map/ppermute | solution.py:23
  36.1 6.7 %collective-permute-start.4 = (bf16[64,2048]{1,0:T(8,128)(2,1)S(1)}, bf16[64,2048]{1,0:T(8,128)(2,1)S(1)}, u32[]{:S(2)}, u32[]{:S(2)}) collective-permute-start(bf16[64,2048]{1,0:T(8,128)(2,1)S(1)} %shard_map.68), channel_id=1, source_target_pairs={{0,2},{2,0},{4,6},{6,4},{1,3},{3,1},{5,7},{7,5},{8,10},{10,8},{12,... | collective-permute-start | bytes 786440 | tf_op jit(solution)/shard_map/ppermute | solution.py:23
  38.5 4.7 %collective-permute-start.11 = (bf16[16,2048]{1,0:T(8,128)(2,1)S(1)}, bf16[16,2048]{1,0:T(8,128)(2,1)S(1)}, u32[]{:S(2)}, u32[]{:S(2)}) collective-permute-start(bf16[16,2048]{1,0:T(8,128)(2,1)S(1)} %shard_map.72), channel_id=1, source_target_pairs={{4,0},{6,2},{0,4},{2,6},{5,1},{7,3},{1,5},{3,7},{12,8},{14,10},{8,... | collective-permute-start | bytes 196616 | tf_op jit(solution)/shard_map/ppermute | solution.py:23
  40.1 6.0 %collective-permute-start.13 = (bf16[16,2048]{1,0:T(8,128)(2,1)S(1)}, bf16[16,2048]{1,0:T(8,128)(2,1)S(1)}, u32[]{:S(2)}, u32[]{:S(2)}) collective-permute-start(bf16[16,2048]{1,0:T(8,128)(2,1)S(1)} %shard_map.74), channel_id=1, source_target_pairs={{4,0},{6,2},{0,4},{2,6},{5,1},{7,3},{1,5},{3,7},{12,8},{14,10},{8,... | collective-permute-start | bytes 196616 | tf_op jit(solution)/shard_map/ppermute | solution.py:23
  40.7 6.4 %collective-permute-start.15 = (bf16[16,2048]{1,0:T(8,128)(2,1)S(1)}, bf16[16,2048]{1,0:T(8,128)(2,1)S(1)}, u32[]{:S(2)}, u32[]{:S(2)}) collective-permute-start(bf16[16,2048]{1,0:T(8,128)(2,1)S(1)} %shard_map.76), channel_id=1, source_target_pairs={{4,0},{6,2},{0,4},{2,6},{5,1},{7,3},{1,5},{3,7},{12,8},{14,10},{8,... | collective-permute-start | bytes 196616 | tf_op jit(solution)/shard_map/ppermute | solution.py:23
  42.3 6.3 %collective-permute-start.17 = (bf16[16,2048]{1,0:T(8,128)(2,1)S(1)}, bf16[16,2048]{1,0:T(8,128)(2,1)S(1)}, u32[]{:S(2)}, u32[]{:S(2)}) collective-permute-start(bf16[16,2048]{1,0:T(8,128)(2,1)S(1)} %shard_map.78), channel_id=1, source_target_pairs={{4,0},{6,2},{0,4},{2,6},{5,1},{7,3},{1,5},{3,7},{12,8},{14,10},{8,... | collective-permute-start | bytes 196616 | tf_op jit(solution)/shard_map/ppermute | solution.py:23
  43.3 6.4 %collective-permute-start.12 = (bf16[16,2048]{1,0:T(8,128)(2,1)S(1)}, bf16[16,2048]{1,0:T(8,128)(2,1)S(1)}, u32[]{:S(2)}, u32[]{:S(2)}) collective-permute-start(bf16[16,2048]{1,0:T(8,128)(2,1)S(1)} %shard_map.73), channel_id=1, source_target_pairs={{24,0},{16,8},{8,16},{0,24},{25,1},{17,9},{9,17},{1,25},{26,2},{18... | collective-permute-start | bytes 196616 | tf_op jit(solution)/shard_map/ppermute | solution.py:23
  46.1 5.7 %collective-permute-start.14 = (bf16[16,2048]{1,0:T(8,128)(2,1)S(1)}, bf16[16,2048]{1,0:T(8,128)(2,1)S(1)}, u32[]{:S(2)}, u32[]{:S(2)}) collective-permute-start(bf16[16,2048]{1,0:T(8,128)(2,1)S(1)} %shard_map.75), channel_id=1, source_target_pairs={{16,0},{24,8},{0,16},{8,24},{17,1},{25,9},{1,17},{9,25},{18,2},{26... | collective-permute-start | bytes 196616 | tf_op jit(solution)/shard_map/ppermute | solution.py:23
  47.1 5.0 %collective-permute-start.16 = (bf16[16,2048]{1,0:T(8,128)(2,1)S(1)}, bf16[16,2048]{1,0:T(8,128)(2,1)S(1)}, u32[]{:S(2)}, u32[]{:S(2)}) collective-permute-start(bf16[16,2048]{1,0:T(8,128)(2,1)S(1)} %shard_map.77), channel_id=1, source_target_pairs={{8,0},{0,8},{24,16},{16,24},{9,1},{1,9},{25,17},{17,25},{10,2},{2,... | collective-permute-start | bytes 196616 | tf_op jit(solution)/shard_map/ppermute | solution.py:23
  (1 other events, 0.7 us)
where the time goes:
time: 53.2 us; the launch traced here: 52.9 us
  starting transfers between devices  22.1 us (42%)
  Pallas kernels  15 us (28%)
  local copies, waits for them, and re-layouts  9.28 us (17%)
  waiting for transfers between devices  5.66 us (11%)
  other arithmetic  0.7 us (1%)
    ppermute x18, starting transfers between devices, move(): lax.ppermute(value, axis, [(d, s) for s, d in pairs] if back else pairs)  22.1 us
    pallas_call x4, Pallas kernels, expert_rows(): pl.pallas_call(functools.partial(expert_kernel, rows), out_shape=jax.Shap...  10.1 us
    unnamed x14, local copies, waits for them, and re-layouts  9.28 us
    ppermute x18, waiting for transfers between devices, move(): lax.ppermute(value, axis, [(d, s) for s, d in pairs] if back else pairs)  5.66 us
    pallas_call x1, Pallas kernels, load_weights(): pl.pallas_call(functools.partial(load_kernel, parts), out_shape=out, in_s...  3.79 us
  transfers between devices with their start and end apart: 18, of which 6 were waited for; matrix products, arithmetic and copies ran while one was open for 0% of the time, Pallas kernels for 28%

commit v1 on v0

--- a/solution.py
+++ b/solution.py
@@ -10,6 +10,7 @@
 CORES = 2
 LANES = 128
 WHOLE_ROWS = 512
+LOAD_MIB = 43
 VMEM = pl.BlockSpec(memory_space=pltpu.VMEM)
 SMEM = pl.BlockSpec(memory_space=pltpu.SMEM)
 HBM = pl.BlockSpec(memory_space=pltpu.HBM)
@@ -23,7 +24,7 @@
     return lax.ppermute(value, axis, [(d, s) for s, d in pairs] if back else pairs)
 
 
-def prep_kernel(ids_ref, gates_ref, tokens_ref, out_ref, ids_held, gates_held, sems):
+def prep_kernel(mine_ref, ids_ref, gates_ref, tokens_ref, out_ref, place_ref, ids_held, gates_held, sems):
     model_width = tokens_ref.shape[1]
     copies = [
         pltpu.make_async_copy(ids_ref, ids_held, sems.at[0]),
@@ -32,6 +33,7 @@
     ]
     for copy in copies:
         copy.start()
+    place_ref[...] = jnp.zeros_like(place_ref) + mine_ref[0]
     copies[0].wait()
     copies[1].wait()
     width = out_ref.shape[1] - model_width
@@ -55,22 +57,35 @@
     copies[2].wait()
 
 
-def prepare(tokens, expert_ids, gate_weights, experts):
+def prepare(mine, tokens, expert_ids, gate_weights, experts):
     rows, model_width = tokens.shape
     top_count = expert_ids.shape[1]
     width = experts + -experts % LANES
     return pl.pallas_call(
         prep_kernel,
-        out_shape=jax.ShapeDtypeStruct((rows, model_width + width), jnp.bfloat16),
-        in_specs=[HBM] * 3,
-        out_specs=VMEM,
+        out_shape=[
+            jax.ShapeDtypeStruct((rows, model_width + width), jnp.bfloat16),
+            jax.ShapeDtypeStruct((8, width), jnp.int32),
+        ],
+        in_specs=[SMEM] + [HBM] * 3,
+        out_specs=[VMEM] * 2,
         scratch_shapes=[
             pltpu.VMEM((top_count, rows), jnp.int32),
             pltpu.VMEM((top_count, rows), jnp.bfloat16),
             pltpu.SemaphoreType.DMA((3,)),
         ],
         compiler_params=pltpu.CompilerParams(vmem_limit_bytes=8 << 20),
-    )(expert_ids.T, gate_weights.T, tokens)
+    )(mine, expert_ids.T, gate_weights.T, tokens)
+
+
+def row_scale(place_ref, table):
+    table = table.astype(jnp.float32)
+    lane = lax.broadcasted_iota(jnp.int32, table.shape, 1)
+    return jnp.sum(jnp.where(lane == place_ref[:1, :], table, 0.0), axis=1, keepdims=True)
+
+
+def activate(gate_pre, up_pre):
+    return (gate_pre / (1.0 + jnp.exp(-gate_pre)) * up_pre).astype(jnp.bfloat16)
 
 
 def load_kernel(parts, *refs):
@@ -103,49 +118,53 @@
         in_specs=[HBM] * len(weights),
         out_specs=[VMEM] * len(out),
         scratch_shapes=[pltpu.SemaphoreType.DMA((parts * len(weights),))],
-        compiler_params=pltpu.CompilerParams(vmem_limit_bytes=43 << 20),
+        compiler_params=pltpu.CompilerParams(vmem_limit_bytes=LOAD_MIB << 20),
         cost_estimate=pl.CostEstimate(
             flops=0, bytes_accessed=sum(w.size for w in weights) * 2, transcendentals=0
         ),
     )(*weights)
 
 
-def expert_kernel(rows, mine_ref, x_ref, gate_ref, up_ref, down_ref, *refs):
-    out_ref = refs[-1]
-    model_width = out_ref.shape[1]
+def expert_kernel(rows, count, place_ref, *refs):
+    inputs, outputs, held = refs[:count], refs[-count - 1 : -1], refs[-1]
+    gate_ref, up_ref, down_ref = refs[count : count + 3]
+    model_width = outputs[0].shape[1]
 
     def body(step, carry):
         part = pl.ds(pl.multiple_of(step * rows, rows), rows)
-        x = x_ref[part, :model_width]
-        table = x_ref[part, model_width:].astype(jnp.float32)
-        lane = lax.broadcasted_iota(jnp.int32, table.shape, 1)
-        scale = jnp.sum(jnp.where(lane == mine_ref[0], table, 0.0), axis=1, keepdims=True)
+        for at, ref in enumerate(inputs):
+            held[at * rows : (at + 1) * rows] = ref[part, :]
+        x = held[:, :model_width]
+        scale = row_scale(place_ref, held[:, model_width:])
         gate_pre = jnp.dot(x, gate_ref[...], preferred_element_type=jnp.float32)
         up_pre = jnp.dot(x, up_ref[...], preferred_element_type=jnp.float32)
-        hidden = (gate_pre / (1.0 + jnp.exp(-gate_pre)) * up_pre).astype(jnp.bfloat16)
-        result = jnp.dot(hidden, down_ref[...], preferred_element_type=jnp.float32)
-        out_ref[part, :] = (result * scale).astype(out_ref.dtype)
+        hidden = activate(gate_pre, up_pre)
+        result = jnp.dot(hidden, down_ref[...], preferred_element_type=jnp.float32) * scale
+        for at, ref in enumerate(outputs):
+            ref[part, :] = result[at * rows : (at + 1) * rows].astype(ref.dtype)
         return carry
 
-    lax.fori_loop(0, x_ref.shape[0] // rows, body, 0)
-
-
-def expert_rows(mine, model_width, weights, x, out_type, *after):
-    total = x.shape[0]
-    rows = next(r for r in range(min(total, 256), 0, -1) if total % r == 0)
-    hidden_width = weights[0].shape[1]
-    return pl.pallas_call(
-        functools.partial(expert_kernel, rows),
-        out_shape=jax.ShapeDtypeStruct((total, model_width), out_type),
-        in_specs=[SMEM] + [VMEM] * 4 + [HBM] * len(after),
-        out_specs=VMEM,
+    lax.fori_loop(0, inputs[0].shape[0] // rows, body, 0)
+
+
+def expert_rows(place, weights, blocks, types, *after):
+    total, width = blocks[0].shape
+    model_width, hidden_width = weights[0].shape
+    count = len(blocks)
+    rows = next(r for r in range(min(total, 128), 0, -1) if total % r == 0 and r % 16 == 0)
+    return pl.pallas_call(
+        functools.partial(expert_kernel, rows, count),
+        out_shape=[jax.ShapeDtypeStruct((total, model_width), kind) for kind in types],
+        in_specs=[VMEM] * (count + 4) + [HBM] * len(after),
+        out_specs=[VMEM] * count,
+        scratch_shapes=[pltpu.VMEM((count * rows, width), jnp.bfloat16)],
         compiler_params=pltpu.CompilerParams(vmem_limit_bytes=16 << 20),
         cost_estimate=pl.CostEstimate(
-            flops=6 * total * model_width * hidden_width,
+            flops=6 * count * total * model_width * hidden_width,
             bytes_accessed=0,
-            transcendentals=total * hidden_width,
+            transcendentals=count * total * hidden_width,
         ),
-    )(mine, x, *weights, *after)
+    )(place, *blocks, *weights, *after)
 
 
 def pack_kernel(count, *refs):
@@ -209,9 +228,8 @@
     def along_core(value):
         return move(value, "exp", [(i, i ^ 1) for i in range(owners)], False)
 
-    own = prepare(tokens, expert_ids, gate_weights, experts)
+    own, place = prepare(mine[None], tokens, expert_ids, gate_weights, experts)
     *weights, loaded = load_weights(w_gate, w_up, w_down)
-    apply = functools.partial(expert_rows, mine[None], model_width, weights)
     width = groups if experts * tok_rows <= WHOLE_ROWS else 1
     total = None
     for first in range(0, groups, width):
@@ -220,14 +238,14 @@
         steps = range(first, first + width)
         line = [along_grp(own, g) if g else own for g in steps]
         far = [along_chip(piece, s) for piece in line for s in range(1, chips)]
-        near = pack(line)
-        near_other = along_core(near)
         far = pack(far, loaded)
         far_other = along_core(far)
-        near_kept = apply(near, jnp.float32)
-        far_back = along_core(apply(far_other, jnp.bfloat16, near_kept))
-        near_back = along_core(apply(near_other, jnp.bfloat16))
-        far_kept = apply(far, jnp.float32)
+        near = pack(line, far_other)
+        near_other = along_core(near)
+        types = (jnp.float32, jnp.bfloat16)
+        far_kept, far_back = expert_rows(place, weights, [far, far_other], types)
+        near_kept, near_back = expert_rows(place, weights, [near, near_other], types, far_kept)
+        far_back, near_back = along_core(far_back), along_core(near_back)
         for at, g in reversed(list(enumerate(steps))):
             terms = []
             for s in range(1, chips):

time: 53.2 us -> 39.4 us (0.74)
  Pallas kernels: 15 us -> 7.18 us
  local copies, waits for them, and re-layouts: 9.28 us -> 2.21 us
  waiting for transfers between devices: 5.66 us -> 6.98 us
    pallas_call x5 -> x3, Pallas kernels: 10.3 us -> 3.21 us  [the longest x2 2.97 us: expert_rows(): pl.pallas_call(functools.partial(expert_kernel, rows, count), out_shape=[...]
    unnamed x14 -> x6, local copies, waits for them, and re-layouts: 9.28 us -> 2.21 us
    ppermute x18, waiting for transfers between devices: 5.66 us -> 6.98 us  [move(): lax.ppermute(value, axis, [(d, s) for s, d in pairs] if back else pairs)]
    pallas_call x2, Pallas kernels: 0.76 us -> 0.05 us  [pack(): pl.pallas_call(functools.partial(pack_kernel, len(pieces)), out_shape=jax...]
  transfers between devices with their start and end apart: 18 -> 18, of which waited for: 6 -> 7; matrix products, arithmetic and copies ran while one was open for 0% -> 0% of each run, Pallas kernels for 28% -> 18%
where the time goes in v1:
time: 39.4 us; the launch traced here: 39.2 us
  starting transfers between devices  22 us (56%)
  Pallas kernels  7.18 us (18%)
  waiting for transfers between devices  6.98 us (18%)
  local copies, waits for them, and re-layouts  2.21 us (6%)
  other arithmetic  0.7 us (2%)
    ppermute x18, starting transfers between devices, move(): lax.ppermute(value, axis, [(d, s) for s, d in pairs] if back else pairs)  22 us
    ppermute x18, waiting for transfers between devices, move(): lax.ppermute(value, axis, [(d, s) for s, d in pairs] if back else pairs)  6.98 us
    pallas_call x1, Pallas kernels, load_weights(): pl.pallas_call(functools.partial(load_kernel, parts), out_shape=out, in_s...  3.79 us
    pallas_call x2, Pallas kernels, expert_rows(): pl.pallas_call(functools.partial(expert_kernel, rows, count), out_shape=[...  2.97 us
    unnamed x6, local copies, waits for them, and re-layouts  2.21 us
  transfers between devices with their start and end apart: 18, of which 7 were waited for; matrix products, arithmetic and copies ran while one was open for 0% of the time, Pallas kernels for 18%

profile of v1, /device:TPU:0, one launch (start us, length us, event | category | flops | bytes accessed | tf_op | source)
XLA Modules:
  0.0 39.2 jit_solution(10698164607222129771)
XLA Ops:
  0.0 0.8 %copy-done = bf16[16,2048]{1,0:T(8,128)(2,1)S(1)} copy-done((bf16[16,2048]{1,0:T(8,128)(2,1)S(1)}, bf16[16,2048]{1,0:T(8,128)(2,1)}, u32[]{:S(2)}) %copy-start) | copy-done | bytes 65560
  0.8 0.7 %copy-done.1 = s32[16,8]{0,1:T(8,128)S(1)} copy-done((s32[16,8]{0,1:T(8,128)S(1)}, s32[16,8]{0,1:T(8,128)}, u32[]{:S(2)}) %copy-start.1) | copy-done | bytes 536
  1.5 0.7 %copy-done.2 = bf16[16,8]{0,1:T(8,128)(2,1)S(1)} copy-done((bf16[16,8]{0,1:T(8,128)(2,1)S(1)}, bf16[16,8]{0,1:T(8,128)(2,1)}, u32[]{:S(2)}) %copy-start.2) | copy-done | bytes 280
  2.5 5.1 %collective-permute-start.2 = (bf16[16,2176]{1,0:T(8,128)(2,1)S(1)}, bf16[16,2176]{1,0:T(8,128)(2,1)S(1)}, u32[]{:S(2)}, u32[]{:S(2)}) collective-permute-start(bf16[16,2176]{1,0:T(8,128)(2,1)S(1)} %get-tuple-element.16.refs_0_), channel_id=1, source_target_pairs={{0,24},{8,16},{16,8},{24,0},{1,25},{9,17},{17,9},{25,1},{2,26},{10... | collective-permute-start | bytes 208904 | tf_op jit(solution)/shard_map/ppermute | solution.py:24
  7.6 0.6 %collective-permute-start = (bf16[16,2176]{1,0:T(8,128)(2,1)S(1)}, bf16[16,2176]{1,0:T(8,128)(2,1)S(1)}, u32[]{:S(2)}, u32[]{:S(2)}) collective-permute-start(bf16[16,2176]{1,0:T(8,128)(2,1)S(1)} %get-tuple-element.16.refs_0_), channel_id=1, source_target_pairs={{0,8},{8,0},{16,24},{24,16},{1,9},{9,1},{17,25},{25,17},{2,10},{10... | collective-permute-start | bytes 208904 | tf_op jit(solution)/shard_map/ppermute | solution.py:24
  8.2 1.7 %collective-permute-start.3 = (bf16[16,2176]{1,0:T(8,128)(2,1)S(1)}, bf16[16,2176]{1,0:T(8,128)(2,1)S(1)}, u32[]{:S(2)}, u32[]{:S(2)}) collective-permute-start(bf16[16,2176]{1,0:T(8,128)(2,1)S(1)} %get-tuple-element.16.refs_0_), channel_id=1, source_target_pairs={{0,4},{2,6},{4,0},{6,2},{1,5},{3,7},{5,1},{7,3},{8,12},{10,14},{12... | collective-permute-start | bytes 208904 | tf_op jit(solution)/shard_map/ppermute | solution.py:24
  10.2 1.9 %collective-permute-start.6 = (bf16[16,2176]{1,0:T(8,128)(2,1)S(1)}, bf16[16,2176]{1,0:T(8,128)(2,1)S(1)}, u32[]{:S(2)}, u32[]{:S(2)}) collective-permute-start(bf16[16,2176]{1,0:T(8,128)(2,1)S(1)} %collective-permute-done.2.refs_3_), channel_id=1, source_target_pairs={{0,4},{2,6},{4,0},{6,2},{1,5},{3,7},{5,1},{7,3},{8,12},{10,14},{12... | collective-permute-start | bytes 208904 | tf_op jit(solution)/shard_map/ppermute | solution.py:24
  12.1 1.4 %collective-permute-done.1.refs_2_ = bf16[16,2176]{1,0:T(8,128)(2,1)S(1)} collective-permute-done((bf16[16,2176]{1,0:T(8,128)(2,1)S(1)}, bf16[16,2176]{1,0:T(8,128)(2,1)S(1)}, u32[]{:S(2)}, u32[]{:S(2)}) %collective-permute-start.1) | collective-permute-done | bytes 69664 | tf_op jit(solution)/shard_map/ppermute | solution.py:24
  13.5 1.5 %collective-permute-start.5 = (bf16[16,2176]{1,0:T(8,128)(2,1)S(1)}, bf16[16,2176]{1,0:T(8,128)(2,1)S(1)}, u32[]{:S(2)}, u32[]{:S(2)}) collective-permute-start(bf16[16,2176]{1,0:T(8,128)(2,1)S(1)} %collective-permute-done.1.refs_2_), channel_id=1, source_target_pairs={{0,4},{2,6},{4,0},{6,2},{1,5},{3,7},{5,1},{7,3},{8,12},{10,14},{12... | collective-permute-start | bytes 208904 | tf_op jit(solution)/shard_map/ppermute | solution.py:24
  15.0 0.5 %collective-permute-start.4 = (bf16[16,2176]{1,0:T(8,128)(2,1)S(1)}, bf16[16,2176]{1,0:T(8,128)(2,1)S(1)}, u32[]{:S(2)}, u32[]{:S(2)}) collective-permute-start(bf16[16,2176]{1,0:T(8,128)(2,1)S(1)} %collective-permute-done.refs_1_), channel_id=1, source_target_pairs={{0,4},{2,6},{4,0},{6,2},{1,5},{3,7},{5,1},{7,3},{8,12},{10,14},{12... | collective-permute-start | bytes 208904 | tf_op jit(solution)/shard_map/ppermute | solution.py:24
  15.5 3.8 %shard_map.65 = (bf16[2048,768]{1,0:T(8,128)(2,1)S(1)}, bf16[2048,768]{1,0:T(8,128)(2,1)S(1)}, bf16[768,2048]{1,0:T(8,128)(2,1)S(1)}, f32[8,128]{1,0:T(8,128)S(1)}) custom-call(bf16[1,2048,768]{2,1,0:T(8,128)(2,1)} %refs_0_.1, bf16[1,2048,768]{2,1,0:T(8,128)(2,1)} %refs_1_.1, bf16[1,768,2048]{2,1,0:T(8,128)(2,1)} %refs_2_.1), custom_call_target="tpu_custom_call" | custom-call | bytes 9437184 | tf_op jit(solution)/shard_map/pallas_call | solution.py:115
  19.5 1.5 %collective-permute-done.7.refs_4_.refs_1_ = bf16[64,2176]{1,0:T(8,128)(2,1)S(1)} collective-permute-done((bf16[64,2176]{1,0:T(8,128)(2,1)S(1)}, bf16[64,2176]{1,0:T(8,128)(2,1)S(1)}, u32[]{:S(2)}, u32[]{:S(2)}) %collective-permute-start.7) | collective-permute-done | bytes 278560 | tf_op jit(solution)/shard_map/ppermute | solution.py:24
  21.2 1.5 %shard_map.68 = (f32[64,2048]{1,0:T(8,128)S(1)}, bf16[64,2048]{1,0:T(8,128)(2,1)S(1)}) custom-call(s32[8,128]{1,0:T(8,128)S(1)} %get-tuple-element.15.place_ref, bf16[64,2176]{1,0:T(8,128)(2,1)S(1)} %shard_map.66.refs_0_, bf16[64,2176]{1,0:T(8,128)(2,1)S(1)} %collective-permute-done.7.refs_4_.refs_1_, bf16[2048,768]{1,0:T(8,128)(2,1)S(1)} %get-tuple-element.18.refs_2_, ...), custom_call_target="tpu_custom_call" | custom-call | flops 1207959552 | tf_op jit(solution)/shard_map/pallas_call | solution.py:155
  23.2 1.5 %shard_map.69 = (f32[64,2048]{1,0:T(8,128)S(1)}, bf16[64,2048]{1,0:T(8,128)(2,1)S(1)}) custom-call(s32[8,128]{1,0:T(8,128)S(1)} %get-tuple-element.15.place_ref, bf16[64,2176]{1,0:T(8,128)(2,1)S(1)} %shard_map.67.refs_0_, bf16[64,2176]{1,0:T(8,128)(2,1)S(1)} %collective-permute-done.8.refs_1_, bf16[2048,768]{1,0:T(8,128)(2,1)S(1)} %get-tuple-element.18.refs_2_, ...), custom_call_target="tpu_custom_call" | custom-call | flops 1207959552 | tf_op jit(solution)/shard_map/pallas_call | solution.py:155
  24.9 1.6 %collective-permute-start.11 = (bf16[16,2048]{1,0:T(8,128)(2,1)S(1)}, bf16[16,2048]{1,0:T(8,128)(2,1)S(1)}, u32[]{:S(2)}, u32[]{:S(2)}) collective-permute-start(bf16[16,2048]{1,0:T(8,128)(2,1)S(1)} %shard_map.70), channel_id=1, source_target_pairs={{4,0},{6,2},{0,4},{2,6},{5,1},{7,3},{1,5},{3,7},{12,8},{14,10},{8,... | collective-permute-start | bytes 196616 | tf_op jit(solution)/shard_map/ppermute | solution.py:24
  26.5 0.6 %collective-permute-start.13 = (bf16[16,2048]{1,0:T(8,128)(2,1)S(1)}, bf16[16,2048]{1,0:T(8,128)(2,1)S(1)}, u32[]{:S(2)}, u32[]{:S(2)}) collective-permute-start(bf16[16,2048]{1,0:T(8,128)(2,1)S(1)} %shard_map.72), channel_id=1, source_target_pairs={{4,0},{6,2},{0,4},{2,6},{5,1},{7,3},{1,5},{3,7},{12,8},{14,10},{8,... | collective-permute-start | bytes 196616 | tf_op jit(solution)/shard_map/ppermute | solution.py:24
  27.1 1.6 %collective-permute-start.15 = (bf16[16,2048]{1,0:T(8,128)(2,1)S(1)}, bf16[16,2048]{1,0:T(8,128)(2,1)S(1)}, u32[]{:S(2)}, u32[]{:S(2)}) collective-permute-start(bf16[16,2048]{1,0:T(8,128)(2,1)S(1)} %shard_map.74), channel_id=1, source_target_pairs={{4,0},{6,2},{0,4},{2,6},{5,1},{7,3},{1,5},{3,7},{12,8},{14,10},{8,... | collective-permute-start | bytes 196616 | tf_op jit(solution)/shard_map/ppermute | solution.py:24
  28.7 0.6 %collective-permute-start.17 = (bf16[16,2048]{1,0:T(8,128)(2,1)S(1)}, bf16[16,2048]{1,0:T(8,128)(2,1)S(1)}, u32[]{:S(2)}, u32[]{:S(2)}) collective-permute-start(bf16[16,2048]{1,0:T(8,128)(2,1)S(1)} %shard_map.76), channel_id=1, source_target_pairs={{4,0},{6,2},{0,4},{2,6},{5,1},{7,3},{1,5},{3,7},{12,8},{14,10},{8,... | collective-permute-start | bytes 196616 | tf_op jit(solution)/shard_map/ppermute | solution.py:24
  29.5 2.9 %collective-permute-start.12 = (bf16[16,2048]{1,0:T(8,128)(2,1)S(1)}, bf16[16,2048]{1,0:T(8,128)(2,1)S(1)}, u32[]{:S(2)}, u32[]{:S(2)}) collective-permute-start(bf16[16,2048]{1,0:T(8,128)(2,1)S(1)} %shard_map.71), channel_id=1, source_target_pairs={{24,0},{16,8},{8,16},{0,24},{25,1},{17,9},{9,17},{1,25},{26,2},{18... | collective-permute-start | bytes 196616 | tf_op jit(solution)/shard_map/ppermute | solution.py:24
  32.4 1.1 %collective-permute-start.14 = (bf16[16,2048]{1,0:T(8,128)(2,1)S(1)}, bf16[16,2048]{1,0:T(8,128)(2,1)S(1)}, u32[]{:S(2)}, u32[]{:S(2)}) collective-permute-start(bf16[16,2048]{1,0:T(8,128)(2,1)S(1)} %shard_map.73), channel_id=1, source_target_pairs={{16,0},{24,8},{0,16},{8,24},{17,1},{25,9},{1,17},{9,25},{18,2},{26... | collective-permute-start | bytes 196616 | tf_op jit(solution)/shard_map/ppermute | solution.py:24
  33.6 1.5 %collective-permute-start.16 = (bf16[16,2048]{1,0:T(8,128)(2,1)S(1)}, bf16[16,2048]{1,0:T(8,128)(2,1)S(1)}, u32[]{:S(2)}, u32[]{:S(2)}) collective-permute-start(bf16[16,2048]{1,0:T(8,128)(2,1)S(1)} %shard_map.75), channel_id=1, source_target_pairs={{8,0},{0,8},{24,16},{16,24},{9,1},{1,9},{25,17},{17,25},{10,2},{2,... | collective-permute-start | bytes 196616 | tf_op jit(solution)/shard_map/ppermute | solution.py:24
  35.0 0.9 %collective-permute-done.12 = bf16[16,2048]{1,0:T(8,128)(2,1)S(1)} collective-permute-done((bf16[16,2048]{1,0:T(8,128)(2,1)S(1)}, bf16[16,2048]{1,0:T(8,128)(2,1)S(1)}, u32[]{:S(2)}, u32[]{:S(2)}) %collective-permute-start.12) | collective-permute-done | bytes 65568 | tf_op jit(solution)/shard_map/ppermute | solution.py:24
  35.9 2.4 %collective-permute-done.14 = bf16[16,2048]{1,0:T(8,128)(2,1)S(1)} collective-permute-done((bf16[16,2048]{1,0:T(8,128)(2,1)S(1)}, bf16[16,2048]{1,0:T(8,128)(2,1)S(1)}, u32[]{:S(2)}, u32[]{:S(2)}) %collective-permute-start.14) | collective-permute-done | bytes 65568 | tf_op jit(solution)/shard_map/ppermute | solution.py:24
  38.5 0.7 %add_add_fusion = f32[16,2048]{1,0:T(8,128)} fusion(bf16[16,2048]{1,0:T(8,128)(2,1)S(1)} %collective-permute-done.17, f32[64,2048]{1,0:T(8,128)S(1)} %get-tuple-element.22.refs_0_, bf16[16,2048]{1,0:T(8,128)(2,1)S(1)} %collective-permute-done.16, bf16[16,2048]{1,0:T(8,128)(2,1)S(1)} %collective-permute-done.14, ...), kind=kLoop, calls=%fused_computation | loop fusion | flops 327680 | bytes 589824 | tf_op jit(solution)/shard_map/add | solution.py:263
  (32 shorter events, 2.1 us)
Async XLA Ops:
  0.0 0.8 %copy-start = (bf16[16,2048]{1,0:T(8,128)(2,1)S(1)}, bf16[16,2048]{1,0:T(8,128)(2,1)}, u32[]{:S(2)}) copy-start(bf16[16,2048]{1,0:T(8,128)(2,1)} %tokens_ref.1) | copy-start | bytes 196612
  0.8 0.7 %copy-start.1 = (s32[16,8]{0,1:T(8,128)S(1)}, s32[16,8]{0,1:T(8,128)}, u32[]{:S(2)}) copy-start(s32[16,8]{0,1:T(8,128)} %param.7) | copy-start | bytes 1540
  1.5 0.7 %copy-start.2 = (bf16[16,8]{0,1:T(8,128)(2,1)S(1)}, bf16[16,8]{0,1:T(8,128)(2,1)}, u32[]{:S(2)}) copy-start(bf16[16,8]{0,1:T(8,128)(2,1)} %param.8) | copy-start | bytes 772
  2.5 7.8 %collective-permute-start.2 = (bf16[16,2176]{1,0:T(8,128)(2,1)S(1)}, bf16[16,2176]{1,0:T(8,128)(2,1)S(1)}, u32[]{:S(2)}, u32[]{:S(2)}) collective-permute-start(bf16[16,2176]{1,0:T(8,128)(2,1)S(1)} %get-tuple-element.16.refs_0_), channel_id=1, source_target_pairs={{0,24},{8,16},{16,8},{24,0},{1,25},{9,17},{17,9},{25,1},{2,26},{10... | collective-permute-start | bytes 208904 | tf_op jit(solution)/shard_map/ppermute | solution.py:24
  7.6 5.9 %collective-permute-start.1 = (bf16[16,2176]{1,0:T(8,128)(2,1)S(1)}, bf16[16,2176]{1,0:T(8,128)(2,1)S(1)}, u32[]{:S(2)}, u32[]{:S(2)}) collective-permute-start(bf16[16,2176]{1,0:T(8,128)(2,1)S(1)} %get-tuple-element.16.refs_0_), channel_id=1, source_target_pairs={{0,16},{8,24},{16,0},{24,8},{1,17},{9,25},{17,1},{25,9},{2,18},{10... | collective-permute-start | bytes 208904 | tf_op jit(solution)/shard_map/ppermute | solution.py:24
  7.6 7.4 %collective-permute-start = (bf16[16,2176]{1,0:T(8,128)(2,1)S(1)}, bf16[16,2176]{1,0:T(8,128)(2,1)S(1)}, u32[]{:S(2)}, u32[]{:S(2)}) collective-permute-start(bf16[16,2176]{1,0:T(8,128)(2,1)S(1)} %get-tuple-element.16.refs_0_), channel_id=1, source_target_pairs={{0,8},{8,0},{16,24},{24,16},{1,9},{9,1},{17,25},{25,17},{2,10},{10... | collective-permute-start | bytes 208904 | tf_op jit(solution)/shard_map/ppermute | solution.py:24
  8.2 11.1 %collective-permute-start.3 = (bf16[16,2176]{1,0:T(8,128)(2,1)S(1)}, bf16[16,2176]{1,0:T(8,128)(2,1)S(1)}, u32[]{:S(2)}, u32[]{:S(2)}) collective-permute-start(bf16[16,2176]{1,0:T(8,128)(2,1)S(1)} %get-tuple-element.16.refs_0_), channel_id=1, source_target_pairs={{0,4},{2,6},{4,0},{6,2},{1,5},{3,7},{5,1},{7,3},{8,12},{10,14},{12... | collective-permute-start | bytes 208904 | tf_op jit(solution)/shard_map/ppermute | solution.py:24
  10.2 9.1 %collective-permute-start.6 = (bf16[16,2176]{1,0:T(8,128)(2,1)S(1)}, bf16[16,2176]{1,0:T(8,128)(2,1)S(1)}, u32[]{:S(2)}, u32[]{:S(2)}) collective-permute-start(bf16[16,2176]{1,0:T(8,128)(2,1)S(1)} %collective-permute-done.2.refs_3_), channel_id=1, source_target_pairs={{0,4},{2,6},{4,0},{6,2},{1,5},{3,7},{5,1},{7,3},{8,12},{10,14},{12... | collective-permute-start | bytes 208904 | tf_op jit(solution)/shard_map/ppermute | solution.py:24
  13.5 5.9 %collective-permute-start.5 = (bf16[16,2176]{1,0:T(8,128)(2,1)S(1)}, bf16[16,2176]{1,0:T(8,128)(2,1)S(1)}, u32[]{:S(2)}, u32[]{:S(2)}) collective-permute-start(bf16[16,2176]{1,0:T(8,128)(2,1)S(1)} %collective-permute-done.1.refs_2_), channel_id=1, source_target_pairs={{0,4},{2,6},{4,0},{6,2},{1,5},{3,7},{5,1},{7,3},{8,12},{10,14},{12... | collective-permute-start | bytes 208904 | tf_op jit(solution)/shard_map/ppermute | solution.py:24
  15.0 4.3 %collective-permute-start.4 = (bf16[16,2176]{1,0:T(8,128)(2,1)S(1)}, bf16[16,2176]{1,0:T(8,128)(2,1)S(1)}, u32[]{:S(2)}, u32[]{:S(2)}) collective-permute-start(bf16[16,2176]{1,0:T(8,128)(2,1)S(1)} %collective-permute-done.refs_1_), channel_id=1, source_target_pairs={{0,4},{2,6},{4,0},{6,2},{1,5},{3,7},{5,1},{7,3},{8,12},{10,14},{12... | collective-permute-start | bytes 208904 | tf_op jit(solution)/shard_map/ppermute | solution.py:24
  19.4 1.6 %collective-permute-start.7 = (bf16[64,2176]{1,0:T(8,128)(2,1)S(1)}, bf16[64,2176]{1,0:T(8,128)(2,1)S(1)}, u32[]{:S(2)}, u32[]{:S(2)}) collective-permute-start(bf16[64,2176]{1,0:T(8,128)(2,1)S(1)} %shard_map.66.refs_0_), channel_id=1, source_target_pairs={{0,2},{2,0},{4,6},{6,4},{1,3},{3,1},{5,7},{7,5},{8,10},{10,8},{12,... | collective-permute-start | bytes 835592 | tf_op jit(solution)/shard_map/ppermute | solution.py:24
  21.0 2.1 %collective-permute-start.8 = (bf16[64,2176]{1,0:T(8,128)(2,1)S(1)}, bf16[64,2176]{1,0:T(8,128)(2,1)S(1)}, u32[]{:S(2)}, u32[]{:S(2)}) collective-permute-start(bf16[64,2176]{1,0:T(8,128)(2,1)S(1)} %shard_map.67.refs_0_), channel_id=1, source_target_pairs={{0,2},{2,0},{4,6},{6,4},{1,3},{3,1},{5,7},{7,5},{8,10},{10,8},{12,... | collective-permute-start | bytes 835592 | tf_op jit(solution)/shard_map/ppermute | solution.py:24
  22.7 2.2 %collective-permute-start.10 = (bf16[64,2048]{1,0:T(8,128)(2,1)S(1)}, bf16[64,2048]{1,0:T(8,128)(2,1)S(1)}, u32[]{:S(2)}, u32[]{:S(2)}) collective-permute-start(bf16[64,2048]{1,0:T(8,128)(2,1)S(1)} %get-tuple-element.24), channel_id=1, source_target_pairs={{0,2},{2,0},{4,6},{6,4},{1,3},{3,1},{5,7},{7,5},{8,10},{10,8},{12,... | collective-permute-start | bytes 786440 | tf_op jit(solution)/shard_map/ppermute | solution.py:24
  24.7 4.8 %collective-permute-start.9 = (bf16[64,2048]{1,0:T(8,128)(2,1)S(1)}, bf16[64,2048]{1,0:T(8,128)(2,1)S(1)}, u32[]{:S(2)}, u32[]{:S(2)}) collective-permute-start(bf16[64,2048]{1,0:T(8,128)(2,1)S(1)} %get-tuple-element.23), channel_id=1, source_target_pairs={{0,2},{2,0},{4,6},{6,4},{1,3},{3,1},{5,7},{7,5},{8,10},{10,8},{12,... | collective-permute-start | bytes 786440 | tf_op jit(solution)/shard_map/ppermute | solution.py:24
  24.9 4.5 %collective-permute-start.11 = (bf16[16,2048]{1,0:T(8,128)(2,1)S(1)}, bf16[16,2048]{1,0:T(8,128)(2,1)S(1)}, u32[]{:S(2)}, u32[]{:S(2)}) collective-permute-start(bf16[16,2048]{1,0:T(8,128)(2,1)S(1)} %shard_map.70), channel_id=1, source_target_pairs={{4,0},{6,2},{0,4},{2,6},{5,1},{7,3},{1,5},{3,7},{12,8},{14,10},{8,... | collective-permute-start | bytes 196616 | tf_op jit(solution)/shard_map/ppermute | solution.py:24
  26.5 5.9 %collective-permute-start.13 = (bf16[16,2048]{1,0:T(8,128)(2,1)S(1)}, bf16[16,2048]{1,0:T(8,128)(2,1)S(1)}, u32[]{:S(2)}, u32[]{:S(2)}) collective-permute-start(bf16[16,2048]{1,0:T(8,128)(2,1)S(1)} %shard_map.72), channel_id=1, source_target_pairs={{4,0},{6,2},{0,4},{2,6},{5,1},{7,3},{1,5},{3,7},{12,8},{14,10},{8,... | collective-permute-start | bytes 196616 | tf_op jit(solution)/shard_map/ppermute | solution.py:24
  27.1 6.4 %collective-permute-start.15 = (bf16[16,2048]{1,0:T(8,128)(2,1)S(1)}, bf16[16,2048]{1,0:T(8,128)(2,1)S(1)}, u32[]{:S(2)}, u32[]{:S(2)}) collective-permute-start(bf16[16,2048]{1,0:T(8,128)(2,1)S(1)} %shard_map.74), channel_id=1, source_target_pairs={{4,0},{6,2},{0,4},{2,6},{5,1},{7,3},{1,5},{3,7},{12,8},{14,10},{8,... | collective-permute-start | bytes 196616 | tf_op jit(solution)/shard_map/ppermute | solution.py:24
  28.7 6.3 %collective-permute-start.17 = (bf16[16,2048]{1,0:T(8,128)(2,1)S(1)}, bf16[16,2048]{1,0:T(8,128)(2,1)S(1)}, u32[]{:S(2)}, u32[]{:S(2)}) collective-permute-start(bf16[16,2048]{1,0:T(8,128)(2,1)S(1)} %shard_map.76), channel_id=1, source_target_pairs={{4,0},{6,2},{0,4},{2,6},{5,1},{7,3},{1,5},{3,7},{12,8},{14,10},{8,... | collective-permute-start | bytes 196616 | tf_op jit(solution)/shard_map/ppermute | solution.py:24
  29.5 6.4 %collective-permute-start.12 = (bf16[16,2048]{1,0:T(8,128)(2,1)S(1)}, bf16[16,2048]{1,0:T(8,128)(2,1)S(1)}, u32[]{:S(2)}, u32[]{:S(2)}) collective-permute-start(bf16[16,2048]{1,0:T(8,128)(2,1)S(1)} %shard_map.71), channel_id=1, source_target_pairs={{24,0},{16,8},{8,16},{0,24},{25,1},{17,9},{9,17},{1,25},{26,2},{18... | collective-permute-start | bytes 196616 | tf_op jit(solution)/shard_map/ppermute | solution.py:24
  32.4 5.9 %collective-permute-start.14 = (bf16[16,2048]{1,0:T(8,128)(2,1)S(1)}, bf16[16,2048]{1,0:T(8,128)(2,1)S(1)}, u32[]{:S(2)}, u32[]{:S(2)}) collective-permute-start(bf16[16,2048]{1,0:T(8,128)(2,1)S(1)} %shard_map.73), channel_id=1, source_target_pairs={{16,0},{24,8},{0,16},{8,24},{17,1},{25,9},{1,17},{9,25},{18,2},{26... | collective-permute-start | bytes 196616 | tf_op jit(solution)/shard_map/ppermute | solution.py:24
  33.6 5.0 %collective-permute-start.16 = (bf16[16,2048]{1,0:T(8,128)(2,1)S(1)}, bf16[16,2048]{1,0:T(8,128)(2,1)S(1)}, u32[]{:S(2)}, u32[]{:S(2)}) collective-permute-start(bf16[16,2048]{1,0:T(8,128)(2,1)S(1)} %shard_map.75), channel_id=1, source_target_pairs={{8,0},{0,8},{24,16},{16,24},{9,1},{1,9},{25,17},{17,25},{10,2},{2,... | collective-permute-start | bytes 196616 | tf_op jit(solution)/shard_map/ppermute | solution.py:24
